TPU v7x, 128 devices: a whole 4x4x4 slice. The times are simulated.
128 devices in a mesh: seq: 16 (over x, y), head: 8 (over z, core).
Axes of the slice: x: 4, y: 4, z: 4, core: 2. Of those that a mesh axis runs over, the one named last changes fastest.
Arguments:
- teacher_queries: bfloat16 [4096, 8192], P('seq', 'head'), may hold values from -5 to 5
- rotated_teacher_keys: bfloat16 [4096, 1024], P('seq', 'head'), may hold values from -5 to 5
- teacher_value_rows: bfloat16 [4096, 1024], P('seq', 'head'), may hold values from -6 to 6
- doc_lengths: int32 [8], replicated, may hold values from 1 to 3072, 4096 in all
- out_proj: bfloat16 [8192, 8192], P('head'), may hold values from -0.0625 to 0.0625
- query_map: float32 [64, 128, 128], P('head'), may hold values from -0.5 to 0.5
- key_map: float32 [64, 128, 128], P('head'), may hold values from -0.5 to 0.5
- beta_weight: float32 [64, 128], P('head'), may hold values from -0.5 to 0.5
- beta_bias: float32 [64], P('head'), may hold values from -5 to 2
Outputs:
- match_loss: float32 [], replicated
- grad_query_map: float32 [64, 128, 128], P('head')
- grad_key_map: float32 [64, 128, 128], P('head')
- grad_beta_weight: float32 [64, 128], P('head')
Inputs may be any that keep to these rules, and one draw needn't show every extreme that they name: `doc_lengths`: the documents lie end to end, in order, and fill the 4096 positions; the longest holds three quarters of them.
All inputs are finite; a program needn't handle non-finite values.
Results may differ from a plain program's by a relative error of at most 0.009.
Values may be sent and summed in bfloat16 or wider, within the bound.
A program may use at most 256 MiB of HBM per device.

v0:
```python
import math

import jax
import jax.numpy as jnp
from jax import lax
from jax.sharding import PartitionSpec as P

HEAD_SIZE = 128
SPAN = 64


highest = lax.Precision.HIGHEST
masked_score = -1e30


def carried_in(value, axis, join, neutral, backward):
    count, mine = (lax.axis_size(axis), lax.axis_index(axis))
    pieces = jax.tree.map(lambda part: lax.all_gather(part, axis), value)
    if backward:
        pieces = jax.tree.map(lambda part: part[::-1], pieces)
        mine = count - 1 - mine
    running = jax.tree.map(
        lambda part, zero: jnp.full_like(part, 0) + jnp.asarray(zero, part.dtype), value, neutral
    )

    def lap(position, running):
        longer = join(running, jax.tree.map(lambda part: part[position], pieces))
        return jax.tree.map(lambda new, old: jnp.where(position < mine, new, old), longer, running)

    return lax.fori_loop(0, count - 1, lap, running)


def doc_index(positions, doc_lengths):
    starts = jnp.cumsum(doc_lengths) - doc_lengths
    inside = (positions[:, None] >= starts[None, 1:]).astype(jnp.int32)
    found_index = jnp.sum(inside, axis=1)
    return jnp.where(positions < 0, -1, found_index)


def unit_rows(tensor):
    activated = jax.nn.silu(tensor)
    return activated / jnp.sqrt(jnp.sum(activated * activated, axis=-1, keepdims=True) + 1e-06)


def features(query_rows, teacher_key_rows, query_map, key_map, beta_weight, beta_bias):
    query_units = unit_rows(jnp.einsum("thd,hde->hte", query_rows, query_map, precision=highest))
    key_units = unit_rows(jnp.einsum("thd,hde->hte", teacher_key_rows, key_map, precision=highest))
    logits = (
        jnp.einsum("thd,hd->ht", query_rows, beta_weight, precision=highest) + beta_bias[:, None]
    )
    return (query_units, key_units, jax.nn.sigmoid(logits))


def span_factors(query_units, key_units, strengths, student_value_rows, same_doc, causal):
    block_length = key_units.shape[-2]
    key_width = key_units.shape[-1]
    identity_block = jnp.eye(block_length, dtype=jnp.float32)
    key_gram = jnp.einsum("...id,...jd->...ij", key_units, key_units, precision=highest)
    coupling = strengths[..., :, None] * key_gram * same_doc * (causal - identity_block)
    system = identity_block + coupling
    right_side = strengths[..., None] * jnp.concatenate([key_units, student_value_rows], axis=-1)
    solved = lax.linalg.triangular_solve(
        system, right_side, left_side=True, lower=True, unit_diagonal=True
    )
    scores = (
        jnp.einsum("...id,...jd->...ij", query_units, key_units, precision=highest)
        * same_doc
        * causal
    )
    return (solved[..., :key_width], solved[..., key_width:], scores)


def span_outputs(query_units, wy_keys, wy_values, scores, starts, lead_flag):
    carried = jnp.einsum("...id,...ed->...ie", query_units, starts, precision=highest)
    removed = jnp.einsum("...jd,...ed->...je", wy_keys, starts, precision=highest)
    carried = carried - jnp.einsum("...ij,...je->...ie", scores, removed, precision=highest)
    fresh_part = jnp.einsum("...ij,...je->...ie", scores, wy_values, precision=highest)
    return lead_flag[..., None] * carried + fresh_part


def matmul_batched(left_side, right_side):
    return jnp.einsum("...ab,...bc->...ac", left_side, right_side, precision=highest)


def compose(earlier, later):
    return (matmul_batched(earlier[0], later[0]), matmul_batched(earlier[1], later[0]) + later[1])


def shards(
    teacher_queries,
    rotated_teacher_keys,
    teacher_value_rows,
    doc_lengths,
    out_proj,
    query_map,
    key_map,
    beta_weight,
    beta_bias,
):
    row_count = teacher_queries.shape[0]
    head_count = query_map.shape[0]
    group_count = rotated_teacher_keys.shape[1] // HEAD_SIZE
    query_group_ratio = head_count // group_count
    span_count = row_count // SPAN
    first_row = lax.axis_index("seq") * row_count
    positions = first_row + jnp.arange(row_count, dtype=jnp.int32)
    doc_ids = doc_index(positions, doc_lengths)
    score_scale = 1.0 / math.sqrt(HEAD_SIZE)
    grouped_queries = teacher_queries.reshape(row_count, group_count, query_group_ratio, HEAD_SIZE)
    key_piece = lax.all_gather(rotated_teacher_keys, "seq", axis=0, tiled=True)
    value_piece = lax.all_gather(teacher_value_rows, "seq", axis=0, tiled=True)
    piece_rows = key_piece.shape[0]
    key_positions = jnp.arange(piece_rows, dtype=jnp.int32)
    allowed = (key_positions[None, :] <= positions[:, None]) & (
        doc_index(key_positions, doc_lengths)[None, :] == doc_ids[:, None]
    )
    row_peak = jnp.full((group_count, query_group_ratio, row_count), masked_score, jnp.float32)
    scores = (
        jnp.einsum(
            "lecu,beu->eclb",
            grouped_queries,
            key_piece.reshape(piece_rows, group_count, HEAD_SIZE),
            preferred_element_type=jnp.float32,
        )
        * score_scale
    )
    scores = jnp.where(allowed, scores, masked_score)
    new_peak = jnp.maximum(row_peak, jnp.max(scores, axis=-1))
    weights = jnp.where(allowed, jnp.exp(scores - new_peak[..., None]), 0.0)
    new_total = jnp.sum(weights, axis=-1)
    new_sum = jnp.einsum(
        "fcuy,yfv->fcuv",
        weights.astype(jnp.bfloat16),
        value_piece.reshape(piece_rows, group_count, HEAD_SIZE),
        preferred_element_type=jnp.float32,
    )
    teacher_out = jnp.transpose(new_sum / new_total[..., None], (2, 0, 1, 3)).reshape(
        row_count, head_count * HEAD_SIZE
    )
    query_rows = teacher_queries.astype(jnp.float32).reshape(row_count, head_count, HEAD_SIZE)
    teacher_key_rows = jnp.repeat(
        rotated_teacher_keys.astype(jnp.float32).reshape(row_count, group_count, HEAD_SIZE),
        query_group_ratio,
        axis=1,
    )
    student_value_rows = jnp.repeat(
        teacher_value_rows.astype(jnp.float32).reshape(row_count, group_count, HEAD_SIZE),
        query_group_ratio,
        axis=1,
    )
    span_docs = doc_ids.reshape(span_count, SPAN)
    before = doc_index(first_row + jnp.arange(span_count, dtype=jnp.int32) * SPAN - 1, doc_lengths)
    lead_flag = (span_docs == before[:, None]).astype(jnp.float32)
    tail_flag = (span_docs == span_docs[:, -1:]).astype(jnp.float32)
    same_doc = (span_docs[:, :, None] == span_docs[:, None, :]).astype(jnp.float32)
    causal = jnp.tril(jnp.ones((SPAN, SPAN), jnp.float32))
    identity_matrix = jnp.eye(HEAD_SIZE, dtype=jnp.float32)
    identity_pair = (
        jnp.broadcast_to(identity_matrix, (head_count, HEAD_SIZE, HEAD_SIZE)),
        jnp.zeros((head_count, HEAD_SIZE, HEAD_SIZE), jnp.float32),
    )

    def blocks(tensor):
        return tensor.reshape((tensor.shape[0], span_count, SPAN) + tensor.shape[2:])

    value_blocks = blocks(jnp.transpose(student_value_rows, (1, 0, 2)))

    def prepare(map_for_queries, map_for_keys, weight_for_beta):
        query_units, key_units, strengths = features(
            query_rows, teacher_key_rows, map_for_queries, map_for_keys, weight_for_beta, beta_bias
        )
        query_units, key_units, strengths = (
            blocks(query_units),
            blocks(key_units),
            blocks(strengths),
        )
        wy_keys, wy_values, scores = span_factors(
            query_units, key_units, strengths, value_blocks, same_doc, causal
        )
        return (query_units, key_units, wy_keys, wy_values, scores)

    def carry_terms(factors):
        query_units, key_units, wy_keys, wy_values, scores = factors
        transitions = lead_flag[None, :, -1, None, None] * (
            identity_matrix - jnp.einsum("hcid,hcie->hcde", wy_keys, key_units, precision=highest)
        )
        additions = jnp.einsum(
            "hcie,hcid->hced", wy_values * tail_flag[None, :, :, None], key_units, precision=highest
        )

        def advance(state_pair, step_pair):
            return (compose(state_pair, step_pair), state_pair)

        last_pair, start_pairs = lax.scan(
            advance, identity_pair, (jnp.moveaxis(transitions, 1, 0), jnp.moveaxis(additions, 1, 0))
        )
        return (start_pairs[0], start_pairs[1], last_pair[0], last_pair[1])

    def emit_rows(factors, products, state_sums, state_in):
        query_units, key_units, wy_keys, wy_values, scores = factors
        starts = jnp.einsum("hed,chdf->hcef", state_in, products, precision=highest) + jnp.moveaxis(
            state_sums, 0, 1
        )
        span_rows = span_outputs(query_units, wy_keys, wy_values, scores, starts, lead_flag)
        return jnp.transpose(
            span_rows.reshape(head_count, row_count, HEAD_SIZE), (1, 0, 2)
        ).reshape(row_count, head_count * HEAD_SIZE)

    factors, back_prepare = jax.vjp(prepare, query_map, key_map, beta_weight)
    (products, state_sums, last_product, last_sum), back_carry = jax.vjp(carry_terms, factors)
    prefix = carried_in((last_product, last_sum), "seq", compose, identity_pair, False)
    state_in = prefix[1]
    student_out, back_emit = jax.vjp(emit_rows, factors, products, state_sums, state_in)
    output_gap = (student_out - teacher_out).astype(jnp.bfloat16)
    row_share = row_count // lax.axis_size("head")
    summed = lax.psum(
        jnp.dot(output_gap, out_proj, preferred_element_type=jnp.float32).astype(jnp.bfloat16),
        "head",
    ).astype(jnp.float32)
    local_rows = lax.dynamic_slice_in_dim(summed, lax.axis_index("head") * row_share, row_share, 0)
    loss_part = jnp.sum(local_rows * local_rows)
    gap_grad = 2.0 * lax.dot_general(
        summed.astype(jnp.bfloat16),
        out_proj,
        (((1,), (1,)), ((), ())),
        preferred_element_type=jnp.float32,
    )
    factor_grads, product_grads, sum_grads, state_grad = back_emit(gap_grad)
    suffix = carried_in(
        (jnp.swapaxes(last_product, 1, 2), state_grad), "seq", compose, identity_pair, True
    )
    adjoint = suffix[1]
    last_grad = jnp.einsum("hed,hef->hdf", state_in, adjoint, precision=highest)
    (carry_grads,) = back_carry((product_grads, sum_grads, last_grad, adjoint))
    query_grad, key_grad, beta_grad = back_prepare(jax.tree.map(jnp.add, factor_grads, carry_grads))
    totals = lax.psum((query_grad, key_grad, beta_grad, loss_part), "seq")
    match_loss = lax.psum(totals[3], "head") / (
        row_count * lax.axis_size("seq") * out_proj.shape[1]
    )
    return (match_loss, totals[0], totals[1], totals[2])


def solution(mesh):
    return jax.shard_map(
        shards,
        mesh=mesh,
        in_specs=(
            P("seq", "head"),
            P("seq", "head"),
            P("seq", "head"),
            P(),
            P("head", None),
            P("head", None, None),
            P("head", None, None),
            P("head", None),
            P("head"),
        ),
        out_specs=(P(), P("head", None, None), P("head", None, None), P("head", None)),
        check_vma=False,
    )
```

profile of v0, /device:TPU:0, one launch (start us, length us, event | category | flops | bytes accessed | tf_op | source)
XLA Modules:
  0.0 912.1 jit_solution(12228154493761620786)
XLA Ops:
  21.1 158.1 %custom-call.7 = f32[8,4,1,64,64]{3,4,2,1,0:T(8,128)S(1)} custom-call(f32[8,4,1,64,64]{4,3,2,1,0:T(8,128)} %add_bitcast_fusion), custom_call_target="InvertDiagBlocksLowerTriangular" | custom-call | tf_op jit(solution)/shard_map/jvp()/triangular_solve | solution.py:62
  194.8 37.3 %while.66 = (s32[]{:T(128)}, f32[8,128,128]{1,2,0:T(8,128)S(1)}, f32[8,128,128]{1,2,0:T(8,128)}, f32[4,8,128,128]{2,3,1,0:T(8,128)}, f32[4,8,128,128]{2,3,1,0:T(...) while((s32[]{:T(128)}, f32[8,128,128]{1,2,0:T(8,128)S(1)}, ...), condition=%wide.region_6.7_spmd.clone, body=%wide.region_5.6_spmd.clone.sunk | while | flops 403046400 | bytes 12058780 | solution.py:194
  243.2 15.2 %fusion.46 = (f32[8,256]{1,0:T(8,128)S(1)}, f32[4096,256,8]{1,0,2:T(8,128)}) fusion(pred[256,4096]{0,1:T(8,128)(4,1)} %fusion.53, bf16[4096,128]{1,0:T(8,128)(2,1)} %all-gather.11.cloned.1.call-done, bf16[256,1024]{1,0:T(8,128)(2,1)S(1)} %copy-done), kind=kOutput, calls=%fused_computation.61 | convolution fusion | flops 2172647424 | bytes 36184064 | tf_op jit(solution)/shard_map/lecu,beu->eclb/dot_general | solution.py:119
  258.4 15.2 %fusion.47 = f32[8,256]{1,0:T(8,128)S(1)} fusion(f32[4096,256,8]{1,0,2:T(8,128)} %get-tuple-element.681, f32[8,256]{1,0:T(8,128)S(1)} %broadcast_maximum_fusion, pred[256,4096]{0,1:T(8,128)(4,1)S(1)} %copy-done.41), kind=kLoop, calls=%fused_computation.62 | loop fusion | flops 41940992 | bytes 34619392 | tf_op jit(solution)/shard_map/reduce_sum | solution.py:130
  273.7 16.4 %fusion.135 = f32[8,256,128]{1,2,0:T(8,128)} fusion(f32[4096,256,8]{1,0,2:T(8,128)} %get-tuple-element.681, f32[8,256]{1,0:T(8,128)S(1)} %broadcast_maximum_fusion, pred[256,4096]{0,1:T(8,128)(4,1)S(1)} %copy-done.41, bf16[4096,128]{0,1:T(8,128)(2,1)} %all-gather.13.cloned.1.call-done, f32[8,256]{1,0:T(8,128)S(1)} %fusion.47), kind=kOutput, calls=%fused_computation.172 | convolution fusion | flops 2189688832 | bytes 36716544 | tf_op jit(solution)/shard_map/fcuy,yfv->fcuv/dot_general | solution.py:131
  290.0 16.3 %all-gather.15.cloned.1.call-done = f32[128,128,128]{2,1,0:T(8,128)} async-done(((f32[8,128,128]{2,1,0:T(8,128)}), f32[128,128,128]{2,1,0:T(8,128)}) %all-gather.15.cloned.1.call-update) | async-done | bytes 8388624 | tf_op jit(solution)/shard_map/all_gather | solution.py:18
  306.4 72.4 %all-gather.17.cloned.1.call-done = f32[128,128,128]{2,1,0:T(8,128)} async-done(((f32[8,128,128]{2,1,0:T(8,128)}), f32[128,128,128]{2,1,0:T(8,128)}) %all-gather.17.cloned.1.call-update) | async-done | bytes 8388624 | tf_op jit(solution)/shard_map/all_gather | solution.py:18
  378.7 51.5 %while.67 = (s32[]{:T(128)}, f32[8,128,128]{1,2,0:T(8,128)S(1)}, s32[]{:T(128)}, f32[16,8,128,128]{3,2,1,0:T(8,128)}, f32[16,8,128,128]{3,2,1,0:T(8,128)}, /*index=5*/s32[]{:T(128)}, s32[]{:T(128)}) while((s32[]{:T(128)}, f32[8,128,128]{1,2,0:T(8,128)S(1)}, s32[]{:T(128)}, f32[16,8,128,128]{3,2,1,0:T(8,128)}, ...), condition=%wide.region_8.9_spmd.clone, body=%wide.region_7.8_spmd.clone.sunk | while | flops 201850880 | bytes 5769323 | solution.py:30
  445.6 12.2 %convolution_convert_fusion = bf16[256,8192]{1,0:T(8,128)(2,1)} fusion(bf16[256,1024]{0,1:T(8,128)(2,1)S(1)} %fusion.110, bf16[1024,8192]{1,0:T(8,128)(2,1)} %param.21), kind=kOutput, calls=%fused_computation.67 | convolution fusion | flops 4297064448 | bytes 21495808 | tf_op jit(solution)/shard_map/dot_general | solution.py:217
  458.8 71.8 %all-reduce.7.cloned.1.call-done = bf16[256,8192]{1,0:T(8,128)(2,1)} async-done(((bf16[256,8192]{1,0:T(8,128)(2,1)}), bf16[256,8192]{1,0:T(8,128)(2,1)}) %all-reduce.7.cloned.1.call-update) | async-done | bytes 4194320 | tf_op jit(solution)/shard_map/psum | solution.py:216
  530.6 12.5 %fusion.81 = f32[32,8,8,128]{3,2,1,0:T(8,128)} fusion(bf16[256,8192]{1,0:T(8,128)(2,1)} %all-reduce.7.cloned.1.call-done, bf16[1024,8192]{1,0:T(8,128)(2,1)} %param.21), kind=kOutput, calls=%fused_computation.104 | convolution fusion | flops 4295229440 | bytes 22020096 | tf_op jit(solution)/shard_map/dot_general | solution.py:222
  559.4 43.8 %all-gather.19.cloned.1.call-done = f32[128,128,128]{2,1,0:T(8,128)} async-done(((f32[8,128,128]{2,1,0:T(8,128)}), f32[128,128,128]{2,1,0:T(8,128)}) %all-gather.19.cloned.1.call-update) | async-done | bytes 8388624 | tf_op jit(solution)/shard_map/all_gather | solution.py:18
  603.2 9.3 %copy.265 = f32[16,8,128,128]{2,3,1,0:T(8,128)} copy(f32[16,8,128,128]{3,2,1,0:T(8,128)} %bitcast.393) | data formatting | bytes 16777216 | tf_op jit(solution)/shard_map/all_gather | solution.py:18
  612.5 8.0 rev.6
  632.4 5.1 fusion.209
  637.5 5.2 fusion.76
  645.7 30.5 %all-gather.21.cloned.1.call-done = f32[128,128,128]{2,1,0:T(8,128)} async-done(((f32[8,128,128]{2,1,0:T(8,128)}), f32[128,128,128]{2,1,0:T(8,128)}) %all-gather.21.cloned.1.call-update) | async-done | bytes 8388624 | tf_op jit(solution)/shard_map/all_gather | solution.py:18
  676.3 9.3 %copy.268 = f32[16,8,128,128]{2,3,1,0:T(8,128)} copy(f32[16,8,128,128]{3,2,1,0:T(8,128)} %bitcast.392) | data formatting | bytes 16777216 | tf_op jit(solution)/shard_map/all_gather | solution.py:18
  685.6 7.7 rev.7
  693.3 29.2 %while.68 = (s32[]{:T(128)}, f32[8,128,128]{1,2,0:T(8,128)S(1)}, s32[]{:T(128)}, f32[16,8,128,128]{2,3,1,0:T(8,128)}, f32[16,8,128,128]{2,3,1,0:T(8,128)}, /*index=5*/s32[]{:T(128)}, s32[]{:T(128)}) while((s32[]{:T(128)}, f32[8,128,128]{1,2,0:T(8,128)S(1)}, s32[]{:T(128)}, f32[16,8,128,128]{2,3,1,0:T(8,128)}, ...), condition=%wide.region_19.20_spmd.clone, body=%wide.region_18.19_spmd.clone.sunk | while | flops 201850880 | bytes 3672679 | solution.py:30
  727.7 51.8 %while.65 = (s32[]{:T(128)}, f32[8,128,128]{1,2,0:T(8,128)}, f32[8,128,128]{1,2,0:T(8,128)S(1)}, f32[4,8,128,128]{3,2,1,0:T(8,128)}, f32[4,8,128,128]{2,3,1,0:T(...) while((s32[]{:T(128)}, f32[8,128,128]{1,2,0:T(8,128)}, ...), condition=%wide.region_21.22_spmd, body=%wide.region_20.21_spmd.sunk | while | flops 805699584 | bytes 13109401 | solution.py:194
  815.4 39.8 %all-reduce.2 = (f32[]{:T(128)}, f32[8,128]{1,0:T(8,128)}) all-reduce(f32[]{:T(128)} %multiply_reduce_fusion.1, f32[8,128]{1,0:T(8,128)S(1)} %bitcast.398), channel_id=1, replica_groups=mesh['seq'=16,'head'=8] {'seq'}, use_global_device_ids=true, to_apply=%region_14.15 | all-reduce | flops 1025 | bytes 8200 | tf_op jit(solution)/shard_map/psum | solution.py:236
  855.1 13.0 %psum.44 = f32[]{:T(128)} all-reduce(f32[]{:T(128)} %get-tuple-element.668), channel_id=1, replica_groups=mesh['seq'=16,'head'=8] {'head'}, use_global_device_ids=true, to_apply=%region_15.16 | all-reduce | flops 1 | bytes 8 | tf_op jit(solution)/shard_map/psum | solution.py:237
  868.8 31.0 %all-reduce.9.cloned.1.call-done = (f32[8,128,128]{1,2,0:T(8,128)}, f32[8,128,128]{1,2,0:T(8,128)}) async-done(((f32[8,128,128]{1,2,0:T(8,128)}, f32[8,128,128]{1,2,0:T(8,128)}), (f32[8,128,128]{1,2,0:T(8,128)}, f32[8,128,128]{1,2,0:T(8,128)})) %all-reduce.9.cloned.1.call-update) | async-done | bytes 1048592 | tf_op jit(solution)/shard_map/psum | solution.py:236
  (404 shorter events, 299.5 us)
Async XLA Ops:
  7.2 11.3 %copy-start = (bf16[256,1024]{1,0:T(8,128)(2,1)S(1)}, bf16[256,1024]{1,0:T(8,128)(2,1)}, u32[]{:S(2)}) copy-start(bf16[256,1024]{1,0:T(8,128)(2,1)} %param.17) | copy-start | bytes 1572868
  7.2 236.1 %all-gather.11.cloned.1.call-start = ((), (), s32[]{:S(2)}) async-start(), calls=%async_computation | async-start | bytes 1114112 | tf_op jit(solution)/shard_map/all_gather | solution.py:110
  7.9 265.7 %all-gather.13.cloned.1.call-start = ((), (), s32[]{:S(2)}) async-start(), calls=%async_computation.1 | async-start | bytes 1114112 | tf_op jit(solution)/shard_map/all_gather | solution.py:111
  9.6 296.8 %all-gather.15.cloned.1.call-start = ((), (), s32[]{:S(2)}) async-start(), calls=%async_computation.3 | async-start | bytes 8912896 | tf_op jit(solution)/shard_map/all_gather | solution.py:18
  10.5 4.8 copy-start.48
  10.6 9.2 %copy-start.45 = (f32[64,64]{1,0:T(8,128)}, f32[64,64]{1,0:T(8,128)S(1)}, u32[]{:S(2)}) copy-start(f32[64,64]{1,0:T(8,128)S(1)} %fusion.188) | copy-start | bytes 49156
  16.2 165.6 %copy-start.59 = (f32[4]{0:T(128)}, f32[4]{0:T(128)S(1)}, u32[]{:S(2)}) copy-start(f32[4]{0:T(128)S(1)} %slice_reduce_fusion.1) | copy-start | bytes 52
  18.4 160.9 %copy-start.47 = (bf16[256,128]{1,0:T(8,128)(2,1)S(1)}, bf16[256,128]{1,0:T(8,128)(2,1)}, u32[]{:S(2)}) copy-start(bf16[256,128]{1,0:T(8,128)(2,1)} %param.19) | copy-start | bytes 196612
  19.7 162.1 %copy-start.43 = (f32[8,4,64]{2,1,0:T(4,128)}, f32[8,4,64]{2,1,0:T(4,128)S(1)}, u32[]{:S(2)}) copy-start(f32[8,4,64]{2,1,0:T(4,128)S(1)} %mul.294) | copy-start | bytes 24580
  19.7 162.1 %copy-start.52 = (pred[64,64]{1,0:T(8,128)(4,1)}, pred[64,64]{1,0:T(8,128)(4,1)S(1)}, u32[]{:S(2)}) copy-start(pred[64,64]{1,0:T(8,128)(4,1)S(1)} %get-tuple-element.690) | copy-start | bytes 12292
  181.8 4.9 copy-start.1
  233.1 145.6 %all-gather.17.cloned.1.call-start = ((), (), s32[]{:S(2)}) async-start(), calls=%async_computation.4 | async-start | bytes 8912896 | tf_op jit(solution)/shard_map/all_gather | solution.py:18
  235.2 295.4 %all-reduce.7.cloned.1.call-start = ((), (), s32[]{:S(2)}) async-start(), calls=%async_computation.2 | async-start | bytes 8388608 | tf_op jit(solution)/shard_map/psum | solution.py:216
  237.8 5.5 copy-start.16
  243.2 15.2 %copy-start.41 = (pred[256,4096]{0,1:T(8,128)(4,1)S(1)}, pred[256,4096]{0,1:T(8,128)(4,1)}, u32[]{:S(2)}) copy-start(pred[256,4096]{0,1:T(8,128)(4,1)} %fusion.53) | copy-start | bytes 3145732
  457.8 145.4 %all-gather.19.cloned.1.call-start = ((), (), s32[]{:S(2)}) async-start(), calls=%async_computation.5 | async-start | bytes 8912896 | tf_op jit(solution)/shard_map/all_gather | solution.py:18
  458.4 217.9 %all-gather.21.cloned.1.call-start = ((), (), s32[]{:S(2)}) async-start(), calls=%async_computation.6 | async-start | bytes 8912896 | tf_op jit(solution)/shard_map/all_gather | solution.py:18
  544.7 83.2 %copy-start.7 = (f32[32,8,8,128]{3,2,0,1:T(8,128)}, f32[32,8,8,128]{3,2,0,1:T(8,128)S(1)}, u32[]{:S(2)}) copy-start(f32[32,8,8,128]{3,2,0,1:T(8,128)S(1)} %copy.408) | copy-start | bytes 3145732
  551.3 5.0 copy-start.11
  559.3 340.5 %all-reduce.9.cloned.1.call-start = ((), (), s32[]{:S(2)}) async-start(), calls=%async_computation.7 | async-start | bytes 2097152 | tf_op jit(solution)/shard_map/psum | solution.py:236
  632.4 5.1 copy-start.10
  632.4 5.1 copy-start.15
  810.0 5.0 copy-start.58
  810.0 5.0 copy-start.62
  (52 other events, 130.3 us)
Sparse Core Ops, SparseCore 0:
  10.2 45.3 all-gather.10
  57.7 44.2 all-gather.12
  233.3 73.0 all-gather.14
  308.4 70.3 all-gather.16
  457.9 72.6 all-reduce.6
  532.6 70.5 all-gather.18
  605.9 70.3 all-gather.20
  813.1 86.7 all-reduce.8
where the time goes:
time: 921 us; the launch traced here: 912 us
  matrix products  278 us (30%)
  waiting for transfers between devices  267 us (29%)
  other arithmetic  193 us (21%)
  local copies, waits for them, and re-layouts  101 us (11%)
  blocking collectives  52.8 us (6%)
  between operations  17.3 us (2%)
    all_gather x4, waiting for transfers between devices, carried_in(): pieces = jax.tree.map(lambda part: lax.all_gather(part, axis), value)  163 us
    another operation x5, other arithmetic, span_factors(): lax.linalg.triangular_solve(system, right_side, left_side=True, lower=Tru...  160 us
    dot_general x54, matrix products, matmul_batched(): jnp.einsum('...ab,...bc->...ac', left_side, right_side, precision=highest)  121 us
    psum x1, waiting for transfers between devices, shards(): lax.psum(jnp.dot(output_gap, out_proj, preferred_element_type=jnp.float32...  71.8 us
    psum x1, blocking collectives, shards(): totals = lax.psum((query_grad, key_grad, beta_grad, loss_part), 'seq')  39.8 us
    psum x1, waiting for transfers between devices, shards(): totals = lax.psum((query_grad, key_grad, beta_grad, loss_part), 'seq')  31 us
    dynamic_slice x30, local copies, waits for them, and re-layouts, lap(): longer = join(running, jax.tree.map(lambda part: part[position], pieces))  19.1 us
    all_gather x2, local copies, waits for them, and re-layouts, carried_in(): pieces = jax.tree.map(lambda part: lax.all_gather(part, axis), value)  18.6 us
  transfers between devices with their start and end apart: 8, of which 6 were waited for; matrix products, arithmetic and copies ran while one was open for 38% of the time, Pallas kernels for 0%

commit v1 on v0

v1 whole, which is shorter than its diff:
```python
import functools
import math

import jax
import jax.numpy as jnp
from jax import lax
from jax.experimental import pallas as pl
from jax.experimental.pallas import tpu as pltpu
from jax.sharding import PartitionSpec as P

HEAD = 128
ROWS = 256
HEADS = 8
SEQ = 16
NDOCS = 8
WIDTH = 8192
HALF = 512
KEY_BLOCK = 2048
TEAM = 4

f32 = jnp.float32
bf16 = jnp.bfloat16
NN = ((1,), (0,))
NT = ((1,), (1,))
TN = ((0,), (0,))
VMEM_BYTES = 56 * 1024 * 1024
MESH = pl.DeviceIdType.MESH


def mm(a, b, dims):
    return lax.dot_general(a, b, (dims, ((), ())), preferred_element_type=f32)


def split(x):
    hi = x.astype(bf16)
    return hi, (x - hi.astype(f32)).astype(bf16)


def d1(a, b, dims):
    return mm(a.astype(bf16), b.astype(bf16), dims)


def d3(a, b, dims):
    ah, al = split(a)
    bh, bl = split(b)
    return mm(ah, bh, dims) + (mm(ah, bl, dims) + mm(al, bh, dims))


def d2(a, b, dims):
    ah, al = split(a)
    return mm(ah, b, dims) + mm(al, b, dims)


def d2r(a, b, dims):
    bh, bl = split(b)
    return mm(a, bh, dims) + mm(a, bl, dims)


def row_starts(lens_ref, first_row):
    t = lax.broadcasted_iota(jnp.int32, (ROWS, 1), 0) + first_row
    start = jnp.zeros((ROWS, 1), jnp.int32)
    at = jnp.int32(0)
    for doc in range(NDOCS):
        start = jnp.where(t >= at, at, start)
        at = at + lens_ref[doc]
    return start - first_row


def iotas():
    return (
        lax.broadcasted_iota(jnp.int32, (ROWS, ROWS), 0),
        lax.broadcasted_iota(jnp.int32, (ROWS, ROWS), 1),
    )


def sigmoid(z):
    return 1.0 / (1.0 + jnp.exp(-z))


def unit(z):
    act = z * sigmoid(z)
    scale = lax.rsqrt(jnp.sum(act * act, axis=-1, keepdims=True) + 1e-06)
    return act * scale


def unit_back(z, grad):
    gate = sigmoid(z)
    act = z * gate
    scale = lax.rsqrt(jnp.sum(act * act, axis=-1, keepdims=True) + 1e-06)
    out = act * scale
    act_grad = scale * (grad - out * jnp.sum(out * grad, axis=-1, keepdims=True))
    return act_grad * (gate * (1.0 + z * (1.0 - gate)))


def lower_inverses(lows, ri, ci):
    half = ROWS // 2
    eye = (ri == ci).astype(f32)
    r, c = ri[:half, :half], ci[:half, :half]
    parts = [p for low in lows for p in (low[:half, :half], low[half:, half:])]
    small = eye[:half, :half]
    near = (r >> 1) == (c >> 1)
    invs = [small - jnp.where(near, p, 0.0) for p in parts]
    parts = [p.astype(bf16) for p in parts]
    for k in range(1, 7):
        ring = ((r >> (k + 1)) == (c >> (k + 1))) & ((r >> k) != (c >> k))
        inv16 = [inv.astype(bf16) for inv in invs]
        mids = [
            mm(jnp.where(ring, p, jnp.zeros_like(p)), i, NN).astype(bf16)
            for p, i in zip(parts, inv16)
        ]
        invs = [inv - mm(i, mid, NN) for inv, i, mid in zip(invs, inv16, mids)]
    whole = []
    for n, low in enumerate(lows):
        top, bottom = invs[2 * n], invs[2 * n + 1]
        corner = -d1(d1(bottom, low[half:, :half], NN), top, NN)
        upper = jnp.concatenate([top, jnp.zeros((half, half), f32)], axis=1)
        lower = jnp.concatenate([corner, bottom], axis=1)
        whole.append(jnp.concatenate([upper, lower], axis=0))
    misses = [(eye - inv) - d3(low, inv, NN) for low, inv in zip(lows, whole)]
    return [inv + d1(inv, miss, NN) for inv, miss in zip(whole, misses)]


def kept(lens_ref, i):
    start = jnp.int32(0)
    at = jnp.int32(0)
    for doc in range(NDOCS):
        start = jnp.where((i + 1) * ROWS > at, at, start)
        at = at + lens_ref[doc]
    return jnp.where(start < i * ROWS, 1.0, 0.0).astype(f32)


def signal_all(peers):
    barrier = pltpu.get_barrier_semaphore()
    for axis, index in peers:
        pl.semaphore_signal(barrier, inc=1, device_id={axis: index}, device_id_type=MESH)
    pl.semaphore_wait(barrier, len(peers))


def seq_peers(me):
    return [("seq", lax.rem(me + hop, SEQ)) for hop in range(1, SEQ)]


def remote(source, target, send_sem, recv_sem, peer, axis="seq"):
    return pltpu.make_async_remote_copy(
        src_ref=source,
        dst_ref=target,
        send_sem=send_sem,
        recv_sem=recv_sem,
        device_id={axis: peer},
        device_id_type=MESH,
    )


def spread(me, source, target, sems, peers):
    send, recv = sems
    for peer in peers:

        @pl.when(peer != me)
        def _(peer=peer):
            remote(source.at[peer], target.at[me], send.at[peer], recv.at[me], peer).start()


def team_peers(me, team):
    return [team * 8 + lax.rem(me + n, 8) for n in range(8)]


def settle(me, source, target, sems):
    send, recv = sems
    for hop in range(1, SEQ):
        peer = lax.rem(me + hop, SEQ)
        remote(source.at[peer], target.at[peer], send.at[peer], recv.at[peer], peer).wait()


def share(me, source, target, sems):
    send, recv = sems
    for hop in range(1, SEQ):
        peer = lax.rem(me + hop, SEQ)
        remote(source, target.at[me], send.at[peer], recv.at[me], peer).start()


def settle_share(me, source, target, sems):
    send, recv = sems
    for hop in range(1, SEQ):
        peer = lax.rem(me + hop, SEQ)
        remote(source, target.at[peer], send.at[peer], recv.at[peer], peer).wait()


def lanes(head):
    return pl.ds(pl.multiple_of(head * HEAD, HEAD), HEAD)


def front_kernel(
    lens_ref, bias_ref, q_ref, k_ref, v_ref, qm_ref, km_ref, bw_ref,
    zq_out, zk_out, beta_out, t_out, w_out, sc_out, qe_out, gap_ref, s_ref, hops_ref,
    zq_ref, zk_ref, beta_ref, t_ref, w_ref, sc_ref, qe_ref, fresh_ref, teacher_ref,
    pa_ref, got, outs, s_in, kv, kk, vv,
    out_sem, kv_send, kv_recv, send1, recv1, send2, recv2,
):
    me = lax.axis_index("seq")
    first = me * ROWS
    k = k_ref[...]
    v16 = v_ref[...]
    v = v16.astype(f32)
    kv[me, :, :HEAD] = k
    kv[me, :, HEAD:] = v16
    signal_all(seq_peers(me))

    def kv_copy(owner, peer):
        return remote(kv.at[owner], kv.at[owner], kv_send.at[peer], kv_recv.at[owner], peer)

    lax.fori_loop(me + 1, SEQ, lambda peer, _: (kv_copy(me, peer).start(), _)[1], 0)

    start = row_starts(lens_ref, first)
    lead = (start < 0).astype(f32)
    lead_last = lead[ROWS - 1 :, :]
    tail = (start == start[ROWS - 1 :, :]).astype(f32)
    ri, ci = iotas()
    allowed = (ci <= ri) & (ci >= start)
    strict = (ci < ri) & (ci >= start)
    team = range(TEAM)

    def prepare(turn, _):
        heads = [turn * TEAM + n for n in team]
        qus, kus, betas = [], [], []
        for h in heads:
            q = q_ref[:, lanes(h)]
            qh, ql = split(qm_ref[h])
            kh, kl = split(km_ref[h])
            zq = mm(q, qh, NN) + mm(q, ql, NN)
            zk = mm(k, kh, NN) + mm(k, kl, NN)
            zq_ref[h] = zq
            zk_ref[h] = zk
            logits = jnp.sum(q.astype(f32) * bw_ref[h], axis=-1, keepdims=True)
            beta = sigmoid(logits + bias_ref[h])
            beta_ref[h] = beta
            qus.append(unit(zq))
            kus.append(unit(zk))
            betas.append(beta)
        lows = [jnp.where(strict, betas[n] * d3(kus[n], kus[n], NT), 0.0) for n in team]
        invs = lower_inverses(lows, ri, ci)
        ws = [
            d3(invs[n], jnp.concatenate([betas[n] * kus[n], betas[n] * v], axis=1), NN)
            for n in team
        ]
        scores = [jnp.where(allowed, d3(qus[n], kus[n], NT), 0.0) for n in team]
        for n, h in enumerate(heads):
            t_ref[h] = invs[n]
            w_ref[h] = ws[n]
            sc_ref[h] = scores[n]
            mixed = d3(scores[n], ws[n], NN)
            qe_ref[h] = qus[n] - mixed[:, :HEAD]
            fresh_ref[h] = mixed[:, HEAD:]
            both = jnp.concatenate([ws[n][:, :HEAD], tail * ws[n][:, HEAD:]], axis=1)
            pair = d3(both, kus[n], TN)
            hop = (-lead_last * pair[:HEAD]).astype(bf16)
            add = pair[HEAD:].astype(bf16)
            for side in range(2):
                pa_ref[2 * h + side, :HEAD] = hop
                pa_ref[2 * h + side, HEAD:] = add[side * (HEAD // 2) : (side + 1) * (HEAD // 2)]
        spread(me, pa_ref, got, (send1, recv1), team_peers(me, turn))
        return _

    lax.fori_loop(0, HEADS // TEAM, prepare, 0)
    kept_arrays = [
        pltpu.make_async_copy(a, b, out_sem.at[n])
        for n, (a, b) in enumerate([
            (zq_ref, zq_out), (zk_ref, zk_out), (beta_ref, beta_out), (t_ref, t_out),
            (w_ref, w_out), (sc_ref, sc_out), (qe_ref, qe_out),
        ])
    ]
    for copy in kept_arrays:
        copy.start()

    def arrive(owner, _):
        kv_copy(owner, owner).wait_recv()
        return _

    lax.fori_loop(0, me, arrive, 0)

    def lay(owner, _):
        at = pl.ds(pl.multiple_of(owner * ROWS, ROWS), ROWS)
        block = kv[owner]
        kk[at, :HEAD] = block[:, :HEAD]
        kk[at, HEAD:] = block[:, :HEAD]
        vv[at, :HEAD] = block[:, HEAD:]
        vv[at, HEAD:] = jnp.ones((ROWS, HEAD), bf16)
        return _

    def blank(owner, _):
        at = pl.ds(pl.multiple_of(owner * ROWS, ROWS), ROWS)
        kk[at, :] = jnp.zeros((ROWS, 2 * HEAD), bf16)
        vv[at, :] = jnp.zeros((ROWS, 2 * HEAD), bf16)
        return _

    lax.fori_loop(0, me + 1, lay, 0)
    lax.fori_loop(me + 1, SEQ, blank, 0)
    scale = math.log2(math.e) / math.sqrt(HEAD)
    row = lax.broadcasted_iota(jnp.int32, (ROWS, 1), 0)
    lane = lax.broadcasted_iota(jnp.int32, (1, KEY_BLOCK), 1)

    def attend(turn):
        queries = []
        for n in team:
            hi, lo = split(q_ref[:, lanes(turn * TEAM + n)].astype(f32) * scale)
            queries.append(jnp.concatenate([hi, lo], axis=1))

        def step(block, carry):
            at = pl.ds(pl.multiple_of(block * KEY_BLOCK, KEY_BLOCK), KEY_BLOCK)
            keys = kk[at, :]
            values = vv[at, :]
            u = lane + (block * KEY_BLOCK - first)
            seen = (u >= start) & (u <= row)
            out = []
            for query, (peak, acc) in zip(queries, carry):
                s = jnp.where(seen, mm(query, keys, NT), -1e30)
                new = jnp.maximum(peak, jnp.max(s, axis=-1, keepdims=True))
                weights = jnp.exp2(s - new).astype(bf16)
                out.append((new, acc * jnp.exp2(peak - new) + mm(weights, values, NN)))
            return tuple(out)

        carry = tuple(
            (jnp.full((ROWS, 1), -1e30, f32), jnp.zeros((ROWS, 2 * HEAD), f32)) for _ in team
        )
        carry = lax.fori_loop(0, (first + ROWS - 1) // KEY_BLOCK + 1, step, carry)
        for n in team:
            acc = carry[n][1]
            teacher_ref[turn * TEAM + n] = acc[:, :HEAD] / acc[:, HEAD : HEAD + 1]

    attend(0)
    got[me] = pa_ref[me]
    settle(me, pa_ref, got, (send1, recv1))

    def advance(i, state):
        outs[i] = state.astype(bf16)
        block = got[i]
        hops_ref[i] = block[:HEAD]
        hop = block[:HEAD]
        return kept(lens_ref, i) * state + d2(state, hop, NN) + block[HEAD:].astype(f32)

    lax.fori_loop(0, SEQ, advance, jnp.zeros((HEAD // 2, HEAD), f32))
    for turn in range(2):
        spread(me, outs, s_in, (send2, recv2), team_peers(me, turn))
    s_in[me] = outs[me]
    attend(1)
    settle(me, outs, s_in, (send2, recv2))
    for h in range(HEADS):
        state = jnp.concatenate([s_in[2 * h], s_in[2 * h + 1]], axis=0)
        s_ref[h] = state
        student = lead * d3(qe_ref[h], state, NT) + fresh_ref[h]
        gap_ref[:, h * HEAD : (h + 1) * HEAD] = (student - teacher_ref[h]).astype(bf16)
    lax.fori_loop(me + 1, SEQ, lambda peer, _: (kv_copy(me, peer).wait_send(), _)[1], 0)
    for copy in kept_arrays:
        copy.wait()


def tail_kernel(
    lens_ref, gap_ref, q_ref, k_ref, v_ref, s_ref, hops_ref,
    proj_ref, zq_in, zk_in, beta_in, t_in, w_in, sc_in, qe_in,
    dq_ref, dk_ref, row_ref, loss_out,
    zq_ref, zk_ref, beta_ref, t_ref, w_ref, sc_ref, qe_ref, grad_ref, loss_ref,
    ds_ref, ds_got, outs, lam_ref, pq, pq_got, pq_own, pq_all, pk, pk_got, pk_own, pk_all,
    w, sib_out, sib_in, far, up, down, in_a, in_b, in_up, in_down, r,
    w_sem, sib_send, sib_recv, rs_send, rs_recv, ag_send, ag_recv, in_sem,
    send1, recv1, send2, recv2, send3, recv3, send4, recv4, send5, recv5, send6, recv6,
):
    me = lax.axis_index("seq")
    head = lax.axis_index("head")
    z, core = head // 2, lax.rem(head, 2)
    zp, zm, z2 = lax.rem(z + 1, 4), lax.rem(z + 3, 4), lax.rem(z + 2, 4)
    above, below, sibling = zp * 2 + core, zm * 2 + core, z * 2 + (1 - core)
    order = (z2, zp, zm, z)

    def weight_copy(side, quarter, half):
        at = side * 8 + quarter * 2 + half
        return pltpu.make_async_copy(
            proj_ref.at[:, pl.ds(pl.multiple_of(at * HALF, HALF), HALF)], w.at[at], w_sem.at[at]
        )

    for side in (1 - core, core):
        for quarter in order:
            for half in range(2):
                weight_copy(side, quarter, half).start()

    kept_arrays = [
        pltpu.make_async_copy(a, b, in_sem.at[n])
        for n, (a, b) in enumerate([
            (qe_in, qe_ref), (zq_in, zq_ref), (zk_in, zk_ref), (w_in, w_ref), (sc_in, sc_ref),
            (beta_in, beta_ref), (t_in, t_ref),
        ])
    ]
    for copy in kept_arrays:
        copy.start()
    signal_all([("head", above), ("head", below), ("head", sibling)] + seq_peers(me))

    def send(source, target, peer, send_sem, recv_sem):
        copy = remote(source, target, send_sem, recv_sem, peer, "head")
        copy.start()
        return copy

    gap = gap_ref[...]

    def part(side, quarter, half):
        weight_copy(side, quarter, half).wait()
        return mm(gap, w[side * 8 + quarter * 2 + half], NN)

    sib = []
    for n, quarter in enumerate(order):
        for half in range(2):
            sib_out[n, half] = part(1 - core, quarter, half).astype(bf16)
        sib.append(send(sib_out.at[n], sib_in.at[n], sibling, sib_send.at[n], sib_recv.at[n]))

    def pair(n, half):
        return part(core, order[n], half) + sib_in[n, half].astype(f32)

    sib[0].wait_recv()
    far[0] = pair(0, 0).astype(bf16)
    send_a = send(far.at[0], in_a, above, rs_send.at[0], rs_recv.at[0])
    far[1] = pair(0, 1).astype(bf16)
    send_b = send(far.at[1], in_b, below, rs_send.at[1], rs_recv.at[1])
    sib[1].wait_recv()
    up[1] = pair(1, 1).astype(bf16)
    first_up = pair(1, 0)
    send_a.wait_recv()
    up[0] = (first_up + in_a[...].astype(f32)).astype(bf16)
    send_up = send(up, in_up, above, rs_send.at[2], rs_recv.at[2])
    sib[2].wait_recv()
    down[0] = pair(2, 0).astype(bf16)
    first_down = pair(2, 1)
    send_b.wait_recv()
    down[1] = (first_down + in_b[...].astype(f32)).astype(bf16)
    send_down = send(down, in_down, below, rs_send.at[3], rs_recv.at[3])
    sib[3].wait_recv()
    mine = [pair(3, 0), pair(3, 1)]
    send_up.wait_recv()
    send_down.wait_recv()
    own = core * 4 + z
    for half in range(2):
        total = mine[half] + (in_up[half].astype(f32) + in_down[half].astype(f32))
        r[own, half] = total.astype(bf16)

    def gather(chunk, half, peer, n):
        ref = r.at[chunk] if half is None else r.at[chunk, half]
        return send(ref, ref, peer, ag_send.at[n], ag_recv.at[n])

    loss_ref[...] = jnp.zeros_like(loss_ref)

    def use(chunk, half, first=False):
        block = r[chunk, half]
        term = 2.0 * mm(block, w[chunk * 2 + half], NT)
        grad_ref[...] = term if first else grad_ref[...] + term
        wide = block.astype(f32)
        loss_ref[...] += jnp.sum(wide * wide, axis=0, keepdims=True)

    sides = core * 4
    others = (1 - core) * 4
    own_up = gather(own, None, above, 0)
    own_down = gather(own, None, below, 1)
    own_sib = gather(own, None, sibling, 2)
    use(own, 0, True)
    use(own, 1)
    own_sib.wait_recv()
    use(others + z, 0)
    use(others + z, 1)
    own_up.wait_recv()
    pass_a = gather(sides + zm, 0, above, 3)
    sib_m = gather(sides + zm, None, sibling, 4)
    own_down.wait_recv()
    pass_b = gather(sides + zp, 1, below, 5)
    sib_p = gather(sides + zp, None, sibling, 6)
    use(sides + zm, 0)
    use(sides + zm, 1)
    use(sides + zp, 0)
    use(sides + zp, 1)
    sib_m.wait_recv()
    use(others + zm, 0)
    use(others + zm, 1)
    sib_p.wait_recv()
    use(others + zp, 0)
    use(others + zp, 1)
    pass_a.wait_recv()
    sib_a = gather(sides + z2, 0, sibling, 7)
    pass_b.wait_recv()
    sib_b = gather(sides + z2, 1, sibling, 8)
    use(sides + z2, 0)
    use(sides + z2, 1)
    sib_a.wait_recv()
    use(others + z2, 0)
    sib_b.wait_recv()
    use(others + z2, 1)
    for copy in sib + [
        send_a, send_b, send_up, send_down, own_up, own_down, own_sib,
        pass_a, sib_m, pass_b, sib_p, sib_a, sib_b,
    ]:
        copy.wait_send()
    for copy in kept_arrays:
        copy.wait()

    start = row_starts(lens_ref, me * ROWS)
    lead = (start < 0).astype(f32)
    lead_last = lead[ROWS - 1 :, :]
    tail = (start == start[ROWS - 1 :, :]).astype(f32)
    ri, ci = iotas()
    allowed = (ci <= ri) & (ci >= start)
    strict = (ci < ri) & (ci >= start)
    team = range(TEAM)
    half = HEAD // 2

    def state_grads(turn, _):
        for n in team:
            h = turn * TEAM + n
            ds = d3(lead * grad_ref[:, lanes(h)], qe_ref[h], TN).astype(bf16)
            ds_ref[2 * h] = ds[:half]
            ds_ref[2 * h + 1] = ds[half:]
        spread(me, ds_ref, ds_got, (send1, recv1), team_peers(me, turn))
        return _

    lax.fori_loop(0, HEADS // TEAM, state_grads, 0)

    def query_side(turn, _):
        heads = [turn * TEAM + n for n in team]
        gs = [grad_ref[:, lanes(h)] for h in heads]
        dqes = [d3(lead * g, s_ref[h], NN) for h, g in zip(heads, gs)]
        boths = [jnp.concatenate([-dqe, g], axis=1) for dqe, g in zip(dqes, gs)]
        dscs = [jnp.where(allowed, d3(b, w_ref[h], NT), 0.0) for h, b in zip(heads, boths)]
        for h, both in zip(heads, boths):
            sc_ref[h] = d3(sc_ref[h], both, TN)
        for n, h in enumerate(heads):
            zq = zq_ref[h]
            qe_ref[h] = d3(dscs[n], unit(zq), TN)
            dqu = dqes[n] + d3(dscs[n], unit(zk_ref[h]), NN)
            dqm = d2r(q_ref[:, lanes(h)], unit_back(zq, dqu), TN)
            pq[2 * h] = dqm[:half]
            pq[2 * h + 1] = dqm[half:]
        spread(me, pq, pq_got, (send3, recv3), team_peers(me, turn))
        return _

    lax.fori_loop(0, HEADS // TEAM, query_side, 0)
    ds_got[me] = ds_ref[me]
    settle(me, ds_ref, ds_got, (send1, recv1))

    def retreat(n, state):
        i = SEQ - 1 - n
        outs[i] = state.astype(bf16)
        return kept(lens_ref, i) * state + d2(state, hops_ref[i], NT) + ds_got[i].astype(f32)

    lax.fori_loop(0, SEQ, retreat, jnp.zeros((half, HEAD), f32))
    for turn in range(2):
        spread(me, outs, lam_ref, (send2, recv2), team_peers(me, turn))
    lam_ref[me] = outs[me]

    pq_got[me] = pq[me]
    settle(me, pq, pq_got, (send3, recv3))
    pq_own[...] = lax.fori_loop(
        0, SEQ, lambda i, total: total + pq_got[i], jnp.zeros((half, HEAD), f32)
    ).astype(bf16)
    share(me, pq_own, pq_all, (send4, recv4))
    pq_all[me] = pq_own[...]
    settle(me, outs, lam_ref, (send2, recv2))

    k = k_ref[...]
    v = v_ref[...].astype(f32)
    loss = jnp.broadcast_to(jnp.sum(loss_ref[...], axis=1, keepdims=True), (1, HEAD))

    def key_side(turn, _):
        heads = [turn * TEAM + n for n in team]
        lams = [jnp.concatenate([lam_ref[2 * h], lam_ref[2 * h + 1]], axis=0) for h in heads]
        kus = [unit(zk_ref[h]) for h in heads]
        ws = [w_ref[h] for h in heads]
        dhops = [lead_last * mm(s_ref[h], lams[n], TN) for n, h in enumerate(heads)]
        drs = []
        for n, h in enumerate(heads):
            dwk = sc_ref[h, :, :HEAD] - d3(kus[n], dhops[n], NT)
            dwv = sc_ref[h, :, HEAD:] + tail * d2(kus[n], lams[n], NT)
            drs.append(d3(t_ref[h], jnp.concatenate([dwk, dwv], axis=1), TN))
        dkus = [
            qe_ref[h]
            - d3(ws[n][:, :HEAD], dhops[n], NN)
            + tail * d2(ws[n][:, HEAD:], lams[n], NN)
            for n, h in enumerate(heads)
        ]
        dlows = [jnp.where(strict, -d3(drs[n], ws[n], NT), 0.0) for n in team]
        kterms = [drs[n][:, :HEAD] + d3(dlows[n], kus[n], NN) for n in team]
        for n, h in enumerate(heads):
            beta = beta_ref[h]
            dbeta = jnp.sum(kterms[n] * kus[n] + drs[n][:, HEAD:] * v, axis=-1, keepdims=True)
            dku = dkus[n] + beta * kterms[n] + d3(beta * dlows[n], kus[n], TN)
            dkm = d2r(k, unit_back(zk_ref[h], dku), TN)
            dlogit = dbeta * beta * (1.0 - beta)
            q = q_ref[:, lanes(h)].astype(f32)
            rows = jnp.concatenate(
                [jnp.sum(q * dlogit, axis=0, keepdims=True), loss, jnp.zeros((14, HEAD), f32)],
                axis=0,
            )
            for side in range(2):
                pk[2 * h + side, :half] = dkm[side * half : (side + 1) * half]
                pk[2 * h + side, half:] = rows
        spread(me, pk, pk_got, (send5, recv5), team_peers(me, turn))
        return _

    lax.fori_loop(0, HEADS // TEAM, key_side, 0)
    pk_got[me] = pk[me]
    settle(me, pk, pk_got, (send5, recv5))
    total = lax.fori_loop(
        0, SEQ, lambda i, total: total + pk_got[i], jnp.zeros((half + 16, HEAD), f32)
    )
    pk_own[...] = total.astype(bf16)
    share(me, pk_own, pk_all, (send6, recv6))
    pk_all[me] = pk_own[...]
    loss_out[...] = total[half:]
    settle_share(me, pq_own, pq_all, (send4, recv4))
    dq_ref[...] = pq_all[...]
    settle_share(me, pk_own, pk_all, (send6, recv6))
    dk_ref[...] = pk_all[:, :half]
    row_ref[...] = pk_all[:, half:]


def shape(dims, dtype):
    return jax.ShapeDtypeStruct(dims, dtype)


SMEM = pl.BlockSpec(memory_space=pltpu.SMEM)
VMEM = pl.BlockSpec(memory_space=pltpu.VMEM)
ANY = pl.BlockSpec(memory_space=pl.ANY)


def params(**more):
    return pltpu.CompilerParams(vmem_limit_bytes=VMEM_BYTES, has_side_effects=True, **more)


def shards(q, k, v, lens, proj, query_map, key_map, beta_weight, beta_bias):
    bw = beta_weight.reshape(HEADS, 1, HEAD)
    square = (HEADS, ROWS, ROWS)
    slab = (HEADS, ROWS, HEAD)
    halves = (SEQ, HEAD // 2, HEAD)
    saved = [slab, slab, (HEADS, ROWS, 1), square, square, square, slab]
    sems = pltpu.SemaphoreType.DMA((SEQ,))
    *saved_arrays, gap, state, hops = pl.pallas_call(
        front_kernel,
        in_specs=[SMEM, SMEM] + [VMEM] * 6,
        out_specs=[ANY] * 7 + [VMEM] * 3,
        out_shape=[shape(dims, f32) for dims in saved] + [
            shape((ROWS, HEADS * HEAD), bf16), shape((HEADS, HEAD, HEAD), bf16),
            shape((SEQ, HEAD, HEAD), bf16),
        ],
        scratch_shapes=[pltpu.VMEM(dims, f32) for dims in saved] + [
            pltpu.VMEM(slab, f32),
            pltpu.VMEM(slab, f32),
            pltpu.VMEM((SEQ, 192, HEAD), bf16),
            pltpu.VMEM((SEQ, 192, HEAD), bf16),
            pltpu.VMEM(halves, bf16),
            pltpu.VMEM(halves, bf16),
            pltpu.VMEM((SEQ, ROWS, 2 * HEAD), bf16),
            pltpu.VMEM((SEQ * ROWS, 2 * HEAD), bf16),
            pltpu.VMEM((SEQ * ROWS, 2 * HEAD), bf16),
            pltpu.SemaphoreType.DMA((7,)),
        ] + [sems] * 6,
        compiler_params=params(collective_id=0),
        name="front",
    )(lens, beta_bias, q, k, v, query_map, key_map, bw)

    block = (2, ROWS, HALF)
    extended = (SEQ, HEAD // 2 + 16, HEAD)
    dq, dk, rows, loss = pl.pallas_call(
        tail_kernel,
        in_specs=[SMEM] + [VMEM] * 6 + [ANY] * 8,
        out_specs=[VMEM] * 4,
        out_shape=[
            shape(halves, bf16), shape(halves, bf16), shape((SEQ, 16, HEAD), bf16),
            shape((16, HEAD), f32),
        ],
        scratch_shapes=[pltpu.VMEM(dims, f32) for dims in saved] + [
            pltpu.VMEM((ROWS, HEADS * HEAD), f32),
            pltpu.VMEM((1, HALF), f32),
            pltpu.VMEM(halves, bf16),
            pltpu.VMEM(halves, bf16),
            pltpu.VMEM(halves, bf16),
            pltpu.VMEM(halves, bf16),
            pltpu.VMEM(halves, f32),
            pltpu.VMEM(halves, f32),
            pltpu.VMEM(halves[1:], bf16),
            pltpu.VMEM(halves, bf16),
            pltpu.VMEM(extended, f32),
            pltpu.VMEM(extended, f32),
            pltpu.VMEM(extended[1:], bf16),
            pltpu.VMEM(extended, bf16),
            pltpu.VMEM((16, HEADS * HEAD, HALF), bf16),
            pltpu.VMEM((4,) + block, bf16),
            pltpu.VMEM((4,) + block, bf16),
            pltpu.VMEM(block, bf16),
            pltpu.VMEM(block, bf16),
            pltpu.VMEM(block, bf16),
            pltpu.VMEM(block[1:], bf16),
            pltpu.VMEM(block[1:], bf16),
            pltpu.VMEM(block, bf16),
            pltpu.VMEM(block, bf16),
            pltpu.VMEM((8,) + block, bf16),
            pltpu.SemaphoreType.DMA((16,)),
            pltpu.SemaphoreType.DMA((4,)),
            pltpu.SemaphoreType.DMA((4,)),
            pltpu.SemaphoreType.DMA((4,)),
            pltpu.SemaphoreType.DMA((4,)),
            pltpu.SemaphoreType.DMA((9,)),
            pltpu.SemaphoreType.DMA((9,)),
            pltpu.SemaphoreType.DMA((7,)),
        ] + [sems] * 12,
        compiler_params=params(collective_id=1),
        name="tail",
    )(lens, gap, q, k, v, state, hops, proj, *saved_arrays)
    match_loss = loss[1, 0] / (SEQ * ROWS * WIDTH)
    grad_query = dq.astype(f32).reshape(HEADS, HEAD, HEAD)
    grad_key = dk.astype(f32).reshape(HEADS, HEAD, HEAD)
    grad_beta = rows[::2, 0].astype(f32)
    return match_loss, grad_query, grad_key, grad_beta


def solution(mesh):
    return jax.shard_map(
        shards,
        mesh=mesh,
        in_specs=(
            P("seq", "head"),
            P("seq", "head"),
            P("seq", "head"),
            P(),
            P("head", None),
            P("head", None, None),
            P("head", None, None),
            P("head", None),
            P("head"),
        ),
        out_specs=(P(), P("head", None, None), P("head", None, None), P("head", None)),
        check_vma=False,
    )
```

time: 921 us -> 174 us (0.19)
  matrix products: 278 us -> 0 us
  waiting for transfers between devices: 267 us -> 0 us
  other arithmetic: 193 us -> 3.42 us
  Pallas kernels: 0 us -> 165 us
  local copies, waits for them, and re-layouts: 101 us -> 1.2 us
  blocking collectives: 52.8 us -> 0 us
  between operations: 17.3 us -> 2.43 us
    dot_general x93 -> x0, matrix products: 271 us -> none  [the longest x54 121 us: matmul_batched(): jnp.einsum('...ab,...bc->...ac', left_side, right_side, precision=highest)]
    pallas_call x0 -> x2, Pallas kernels: none -> 165 us  [the longest x1 103 us: shards(): pl.pallas_call(tail_kernel, in_specs=[SMEM] + [VMEM] * 6 + [ANY] * 8, out...]
    all_gather x6 -> x0, waiting for transfers between devices: 163 us -> none  [the longest x4 163 us: carried_in(): pieces = jax.tree.map(lambda part: lax.all_gather(part, axis), value)]
    another operation x7 -> x0, other arithmetic: 160 us -> none  [the longest x5 160 us: span_factors(): lax.linalg.triangular_solve(system, right_side, left_side=True, lower=Tru...]
    psum x2 -> x0, waiting for transfers between devices: 103 us -> none  [the longest x1 71.8 us: shards(): lax.psum(jnp.dot(output_gap, out_proj, preferred_element_type=jnp.float32...]
    psum x2 -> x0, blocking collectives: 52.8 us -> none  [the longest x1 39.8 us: shards(): totals = lax.psum((query_grad, key_grad, beta_grad, loss_part), 'seq')]
    dynamic_slice x46 -> x0, local copies, waits for them, and re-layouts: 29.3 us -> none  [the longest x30 19.1 us: lap(): longer = join(running, jax.tree.map(lambda part: part[position], pieces))]
    reduce_sum x7 -> x0, other arithmetic: 19.1 us -> none  [the longest x1 15.2 us: shards(): new_total = jnp.sum(weights, axis=-1)]
  transfers between devices with their start and end apart: 8 -> 0, of which waited for: 6 -> 0; matrix products, arithmetic and copies ran while one was open for 38% -> 0% of each run, Pallas kernels for 0% -> 0%
where the time goes in v1:
time: 174 us; the launch traced here: 172 us
  Pallas kernels  165 us (95%)
  other arithmetic  3.42 us (2%)
  between operations  2.43 us (1%)
    pallas_call x1, Pallas kernels, shards(): pl.pallas_call(tail_kernel, in_specs=[SMEM] + [VMEM] * 6 + [ANY] * 8, out...  103 us
    pallas_call x1, Pallas kernels, shards(): pl.pallas_call(front_kernel, in_specs=[SMEM, SMEM] + [VMEM] * 6, out_spec...  61.1 us

profile of v1, /device:TPU:0, one launch (start us, length us, event | category | flops | bytes accessed | tf_op | source)
XLA Modules:
  0.0 171.6 jit_solution(15471532926171444981)
XLA Ops:
  0.6 61.1 %front.1 = (f32[8,256,128]{2,1,0:T(8,128)}, f32[8,256,128]{2,1,0:T(8,128)}, f32[8,256,1]{2,1,0:T(8,128)}, f32[8,256,256]{2,1,0:T(8,128)}, f32[8,256,256]{2,1,0:T...) custom-call(s32[8]{0:T(128)} %lens_ref.3, ...), custom_call_target="tpu_custom_call" | custom-call | tf_op jit(solution)/shard_map/front/pallas_call | solution.py:637
  61.7 103.5 %tail.1 = (bf16[16,64,128]{2,1,0:T(8,128)(2,1)}, bf16[16,64,128]{2,1,0:T(8,128)(2,1)}, bf16[16,16,128]{2,1,0:T(8,128)(2,1)}, f32[16,128]{1,0:T(8,128)}) custom-call(s32[8]{0:T(128)} %lens_ref.3, bf16[256,1024]{1,0:T(8,128)(2,1)} %get-tuple-element.18.gap_ref, bf16[256,1024]{1,0:T(8,128)(2,1)} %q_ref.3, bf16[256,128]{1,0:T(8,128)(2,1)} %k_ref.3, ...), custom_call_target="tpu_custom_call" | custom-call | tf_op jit(solution)/shard_map/tail/pallas_call | solution.py:663
  165.2 1.2 slice.6
  167.0 1.3 slice_convert_fusion
  168.3 2.1 %bitcast_convert_fusion = (f32[8,128,128]{2,1,0:T(8,128)}, f32[8,128,128]{2,1,0:T(8,128)}) fusion(bf16[8,128,128]{2,1,0:T(8,128)(2,1)} %bitcast.11, bf16[8,128,128]{2,1,0:T(8,128)(2,1)} %bitcast.10), kind=kLoop, calls=%fused_computation | loop fusion | flops 262144 | bytes 1572864 | tf_op jit(solution)/shard_map/reshape | solution.py:711
